TPU v7x, 32 devices: a whole 2x2x4 slice. The times are simulated.
32 devices in a mesh: groups: 2 (over y), cache: 4 (over z), req: 2 (over x), rep: 2 (over core).
Axes of the slice: x: 2, y: 2, z: 4, core: 2. Of those that a mesh axis runs over, the one named last changes fastest.
Arguments:
- candidates: bfloat16 [16, 512, 4, 1024], P(('groups', 'cache', 'req'), None, None, 'rep'), parts along dimension 0, may hold values from -6 to 6
- kv_cache: bfloat16 [256, 2, 64, 1024], P(('groups', 'cache', 'req'), None, None, 'rep'), parts along dimension 0, may hold values from -6 to 6
- tile_owner: int32 [16, 16], P(('groups', 'cache', 'req')), parts along dimension 0, may hold values from 0 to 3, as said below
- tile_slot: int32 [16, 16], P(('groups', 'cache', 'req')), parts along dimension 0, may hold values from 0 to 15
- tile_length: int32 [16, 16], P(('groups', 'cache', 'req')), parts along dimension 0, may hold values from 0 to 64, as said below
- norm_gain: float32 [1024], P('rep'), may hold values from 0.5 to 1.5
Outputs:
- gated: bfloat16 [16, 512, 1024], P(('groups', 'cache', 'req'), None, 'rep'), parts along dimension 0
There are 2 independent parts, one for each index of `groups`. A program takes and returns all parts, laid end to end along the dimension named above; an argument that names none is the same for every part. Nothing has to cross between parts.
Inputs may be any that keep to these rules, and one draw needn't show every extreme that they name: `tile_owner`: among one request's entries of positive tile_length, no owner is named more than 5 times, and one owner exactly 5 times. `tile_length`: an entry of length 0 is padding; every request has an entry of length 64.
All inputs are finite; a program needn't handle non-finite values.
Results may differ from a plain program's by a relative error of at most 0.0066.
Values may be sent and summed in bfloat16 or wider, within the bound.
A program may use at most 64 MiB of HBM per device.

v0:
```python
import math

import jax
import jax.numpy as jnp
from jax import lax
from jax.sharding import PartitionSpec as P

D = 1024
HEADS = 8
TILE = 64
HT = 16


def attend(query_rows, key_rows, value_rows, live_mask, scaling):
    scores = (
        jnp.einsum("che,khe->hck", query_rows, key_rows, preferred_element_type=jnp.float32)
        * scaling
    )
    weights = (jax.nn.silu(scores) * live_mask[None, None, :]).astype(jnp.bfloat16)
    return jnp.einsum("hck,khe->che", weights, value_rows, preferred_element_type=jnp.float32)


def tile_block(query_rows, tile_data, lengths, scaling):
    heads_here = query_rows.shape[1]
    head_width = query_rows.shape[2]
    positions = jnp.arange(tile_data.shape[2], dtype=jnp.int32)
    live_mask = (positions[None, :] < lengths[:, None]).reshape(-1).astype(jnp.float32)
    key_rows = tile_data[:, 0].reshape(-1, heads_here, head_width)
    value_rows = tile_data[:, 1].reshape(-1, heads_here, head_width)
    return attend(query_rows, key_rows, value_rows, live_mask, scaling)


def pick_table(owners, lengths, wanted, slot_depth):
    owned_mask = ((owners == wanted[:, None]) & (lengths > 0)).astype(jnp.int32)
    rank_order = jnp.cumsum(owned_mask, axis=-1) - 1
    levels = jnp.arange(slot_depth, dtype=jnp.int32)
    return owned_mask[:, None, :] * (rank_order[:, None, :] == levels[None, :, None]).astype(
        jnp.int32
    )


def local(candidates, kv_cache, tile_owner, tile_slot, tile_length, norm_gain):
    cache_size = lax.axis_size("cache")
    slot_depth = (HT - 2) // cache_size + 2
    head_dim = D // HEADS
    scaling = 1.0 / math.sqrt(head_dim)
    cand_rows = candidates.shape[1]
    local_width = candidates.shape[3]
    heads_here = local_width // head_dim
    activated = jax.nn.silu(candidates[0].astype(jnp.float32)).astype(jnp.bfloat16)
    query_rows = activated[:, 0].reshape(cand_rows, heads_here, head_dim)
    all_owner, all_slot, all_length = (
        lax.all_gather(tile_owner, "cache", axis=0, tiled=True),
        lax.all_gather(tile_slot, "cache", axis=0, tiled=True),
        lax.all_gather(tile_length, "cache", axis=0, tiled=True),
    )
    my_index = lax.axis_index("cache")
    senders = jnp.arange(cache_size, dtype=jnp.int32)
    serve_table = pick_table(
        all_owner, all_length, jnp.full((cache_size,), my_index, jnp.int32), slot_depth
    )
    send_slot = jnp.sum(serve_table * all_slot[:, None, :], axis=-1)
    own_owner = jnp.broadcast_to(tile_owner, (cache_size, tile_owner.shape[1]))
    own_length = jnp.broadcast_to(tile_length, (cache_size, tile_length.shape[1]))
    home_table = pick_table(own_owner, own_length, senders, slot_depth)
    home_length = jnp.sum(home_table * own_length[:, None, :], axis=-1)
    outgoing = kv_cache[send_slot]
    arrived = lax.all_to_all(outgoing, "cache", split_axis=0, concat_axis=0, tiled=True)

    def add_owner(owner_index, running):
        return running + tile_block(
            query_rows, arrived[owner_index], home_length[owner_index], scaling
        )

    history = lax.fori_loop(0, cache_size, add_owner, jnp.zeros(query_rows.shape, jnp.float32))
    own_key = activated[:, 1].reshape(cand_rows, heads_here, head_dim).astype(jnp.float32)
    own_value = activated[:, 2].reshape(cand_rows, heads_here, head_dim).astype(jnp.float32)
    own_score = jnp.sum(query_rows.astype(jnp.float32) * own_key, axis=-1) * scaling
    attended = (
        (history + jax.nn.silu(own_score)[:, :, None] * own_value) / (HT * TILE + 1)
    ).reshape(cand_rows, local_width)
    row_sums, squares = lax.psum(
        (jnp.sum(attended, axis=-1), jnp.sum(attended * attended, axis=-1)), "rep"
    )
    average = row_sums / D
    spread = squares / D - average * average
    normed = (attended - average[:, None]) * lax.rsqrt(spread[:, None] + 1e-05) * norm_gain
    gated = (normed * activated[:, 3].astype(jnp.float32)).astype(jnp.bfloat16)
    return gated[None]


def solution(mesh):
    placed = (
        P(("groups", "cache", "req"), None, None, "rep"),
        P(("groups", "cache", "req"), None, None, "rep"),
        P(("groups", "cache", "req"), None),
        P(("groups", "cache", "req"), None),
        P(("groups", "cache", "req"), None),
        P("rep"),
    )
    return jax.shard_map(
        local,
        mesh=mesh,
        in_specs=placed,
        out_specs=P(("groups", "cache", "req"), None, "rep"),
        check_vma=False,
    )
```

profile of v0, /device:TPU:1, one launch (start us, length us, event | category | flops | bytes accessed | tf_op | source)
XLA Modules:
  0.0 121.1 jit_solution(18203352101379214747)
XLA Ops:
  0.0 10.2 %all-gather.2 = s32[4,1,16]{2,1,0:T(1,128)S(1)} all-gather(s32[1,1,16]{2,1,0:T(1,128)} %bitcast.81), channel_id=1, replica_groups=mesh['groups'=2,'cache'=4,'req'=2,'rep'=2] {'cache'}, dimensions={0}, use_global_device_ids=true | all-gather | bytes 320 | tf_op jit(solution)/shard_map/all_gather | solution.py:54
  10.2 6.0 %all-gather.1 = s32[4,1,16]{2,1,0:T(1,128)S(1)} all-gather(s32[1,1,16]{2,1,0:T(1,128)} %bitcast.77), channel_id=1, replica_groups=mesh['groups'=2,'cache'=4,'req'=2,'rep'=2] {'cache'}, dimensions={0}, use_global_device_ids=true | all-gather | bytes 320 | tf_op jit(solution)/shard_map/all_gather | solution.py:55
  16.2 7.3 %all-gather = s32[4,1,16]{2,1,0:T(1,128)S(1)} all-gather(s32[1,1,16]{2,1,0:T(1,128)} %bitcast.79), channel_id=1, replica_groups=mesh['groups'=2,'cache'=4,'req'=2,'rep'=2] {'cache'}, dimensions={0}, use_global_device_ids=true | all-gather | bytes 320 | tf_op jit(solution)/shard_map/all_gather | solution.py:53
  23.5 0.2 reduce_window_sum.17
  23.7 0.2 multiply_reduce_fusion.3
  23.9 0.1 copy.44
  24.0 0.1 reshape.227
  24.1 2.4 %gather_fusion = bf16[20,2,64,512]{3,2,1,0:T(8,128)(2,1)} fusion(bf16[16,2,64,512]{3,2,1,0:T(8,128)(2,1)S(1)} %copy-done, s32[1024]{0:T(1024)S(1)} %pad_clamp_fusion), kind=kCustom, calls=%fused_computation | custom fusion | bytes 5242960 | tf_op jit(solution)/shard_map/gather | solution.py:67
  26.5 4.7 %all-to-all-start = ((bf16[4,5,2,64,512]{4,3,2,1,0:T(8,128)(2,1)}), bf16[4,5,2,64,512]{4,3,2,1,0:T(8,128)(2,1)}, u32[]{:S(2)}, u32[]{:S(2)}) async-start(bf16[4,5,2,64,512]{4,3,2,1,0:T(8,128)(2,1)} %bitcast.71), calls=%async_computation | async-start | bytes 5242880 | tf_op jit(solution)/shard_map/all_to_all | solution.py:68
  31.2 0.2 reduce_window_sum.18
  31.4 0.2 multiply_reduce_fusion.2
  31.6 0.1 copy.48
  31.7 3.0 %fusion.18 = bf16[512,4,512]{2,0,1:T(8,128)(2,1)S(1)} fusion(bf16[1,512,4,512]{3,2,1,0:T(4,128)(2,1)} %param.8), kind=kLoop, calls=%fused_computation.27 | loop fusion | flops 6291456 | bytes 4194304 | tf_op jit(solution)/shard_map/convert_element_type | solution.py:50
  34.7 1.4 %copy-done.1 = bf16[512,4,512]{2,0,1:T(8,128)(2,1)} copy-done((bf16[512,4,512]{2,0,1:T(8,128)(2,1)}, bf16[512,4,512]{2,0,1:T(8,128)(2,1)S(1)}, u32[]{:S(2)}) %copy-start.1) | copy-done | bytes 2097176
  36.1 1.5 %slice_convert_fusion.1 = (f32[512,1,512]{2,0,1:T(8,128)S(1)}, f32[512,1,512]{2,0,1:T(8,128)}, bf16[512,1,512]{2,0,1:T(8,128)(2,1)}) fusion(bf16[512,4,512]{2,0,1:T(8,128)(2,1)S(1)} %fusion.18), kind=kLoop, calls=%fused_computation.35 | loop fusion | flops 524288 | bytes 4194304 | tf_op jit(solution)/shard_map/convert_element_type | solution.py:76
  37.5 1.3 %reshape.222 = f32[512,4,128]{2,1,0:T(4,128)} reshape(f32[512,1,512]{2,0,1:T(8,128)S(1)} %get-tuple-element.165) | data formatting | bytes 2097152 | tf_op jit(solution)/shard_map/convert_element_type | solution.py:76
  38.9 1.2 reshape_squeeze.2
  40.0 0.9 copy.47
  40.9 1.9 %multiply_reduce_fusion.1 = f32[512,4]{1,0:T(8,128)S(1)} fusion(f32[512,4,128]{2,1,0:T(4,128)} %reshape.222, bf16[512,4,128]{2,1,0:T(4,128)(2,1)S(1)} %reshape_squeeze.2), kind=kLoop, calls=%fused_computation.32 | loop fusion | flops 784384 | bytes 1581056 | tf_op jit(solution)/shard_map/reduce_sum | solution.py:78
  42.8 0.1 copy.49
  42.9 2.5 %copy.52 = f32[512,1,512]{0,2,1:T(8,128)} copy(f32[512,1,512]{2,0,1:T(8,128)} %get-tuple-element.166) | data formatting | bytes 2097152 | tf_op jit(solution)/shard_map/convert_element_type | solution.py:77
  45.4 44.7 %all-to-all-done = bf16[4,5,2,64,512]{4,3,2,1,0:T(8,128)(2,1)} async-done(((bf16[4,5,2,64,512]{4,3,2,1,0:T(8,128)(2,1)}), bf16[4,5,2,64,512]{4,3,2,1,0:T(8,128)(2,1)}, u32[]{:S(2)}, u32[]{:S(2)}) %all-to-all-start) | async-done | bytes 2621472 | tf_op jit(solution)/shard_map/all_to_all | solution.py:68
  90.2 20.9 %while.14 = (s32[]{:T(128)}, f32[512,4,128]{0,2,1:T(8,128)}, bf16[4,5,2,64,512]{4,3,2,1,0:T(8,128)(2,1)}, bf16[512,4,128]{2,0,1:T(8,128)(2,1)}, s32[4,5]{1,0:T(4,128)S(1)}, /*index=5*/s32[]{:T(128)}, s32[]{:T(128)}) while((s32[]{:T(128)}, f32[512,4,128]{0,2,1:T(8,128)}, bf16[4,5,2,64,512]{4,3,2,1,0:T(8,128)(2,1)}, ...), condition=%wide.region_5.6_spmd.clone, body=%wide.region_4.5_spmd.clone.sunk | while | flops 340656768 | bytes 7214243 | solution.py:75
  90.2 0.1 fusion.34
  90.2 0.1 reshape.248
  90.3 1.1 copy_bitcast_fusion.2
  91.5 0.1 squeeze.31
  91.6 0.1 squeeze.32
  91.7 3.4 %fusion.36 = f32[512,4,128]{0,2,1:T(8,128)} fusion(bf16[512,4,128]{2,0,1:T(8,128)(2,1)} %get-tuple-element.222, f32[320]{0:T(512)S(1)} %reshape.248, f32[512,4,128]{0,2,1:T(8,128)} %get-tuple-element.213, pred[]{:T(512)S(6)} %compare.3, bf16[320,4,128]{2,1,0:T(4,128)(2,1)S(1)} %squeeze.31, bf16[320,4,128]{2,1,0:T(4,128)(2,1)S(1)} %squeeze.32), kind=kOutput, calls=%fused_computation.9.clone.1 | convolution fusion | flops 340656128 | bytes 3278081 | tf_op jit(solution)/shard_map/while/body/eval_jaxpr/hck,khe->che/dot_general | solution.py:20
  95.2 0.1 reshape.248
  95.3 1.1 copy_bitcast_fusion.2
  96.5 0.1 squeeze.31
  96.6 0.1 squeeze.32
  96.7 3.8 %fusion.36 = f32[512,4,128]{0,2,1:T(8,128)} fusion(bf16[512,4,128]{2,0,1:T(8,128)(2,1)} %get-tuple-element.222, f32[320]{0:T(512)S(1)} %reshape.248, f32[512,4,128]{0,2,1:T(8,128)} %get-tuple-element.213, pred[]{:T(512)S(6)} %compare.3, bf16[320,4,128]{2,1,0:T(4,128)(2,1)S(1)} %squeeze.31, bf16[320,4,128]{2,1,0:T(4,128)(2,1)S(1)} %squeeze.32), kind=kOutput, calls=%fused_computation.9.clone.1 | convolution fusion | flops 340656128 | bytes 3278081 | tf_op jit(solution)/shard_map/while/body/eval_jaxpr/hck,khe->che/dot_general | solution.py:20
  100.5 0.1 reshape.248
  100.6 1.1 copy_bitcast_fusion.2
  101.8 0.1 squeeze.31
  101.9 0.1 squeeze.32
  102.0 3.8 %fusion.36 = f32[512,4,128]{0,2,1:T(8,128)} fusion(bf16[512,4,128]{2,0,1:T(8,128)(2,1)} %get-tuple-element.222, f32[320]{0:T(512)S(1)} %reshape.248, f32[512,4,128]{0,2,1:T(8,128)} %get-tuple-element.213, pred[]{:T(512)S(6)} %compare.3, bf16[320,4,128]{2,1,0:T(4,128)(2,1)S(1)} %squeeze.31, bf16[320,4,128]{2,1,0:T(4,128)(2,1)S(1)} %squeeze.32), kind=kOutput, calls=%fused_computation.9.clone.1 | convolution fusion | flops 340656128 | bytes 3278081 | tf_op jit(solution)/shard_map/while/body/eval_jaxpr/hck,khe->che/dot_general | solution.py:20
  105.8 0.1 reshape.248
  105.9 1.1 copy_bitcast_fusion.2
  107.1 0.1 squeeze.31
  107.2 0.1 squeeze.32
  107.3 3.8 %fusion.36 = f32[512,4,128]{0,2,1:T(8,128)} fusion(bf16[512,4,128]{2,0,1:T(8,128)(2,1)} %get-tuple-element.222, f32[320]{0:T(512)S(1)} %reshape.248, f32[512,4,128]{0,2,1:T(8,128)} %get-tuple-element.213, pred[]{:T(512)S(6)} %compare.3, bf16[320,4,128]{2,1,0:T(4,128)(2,1)S(1)} %squeeze.31, bf16[320,4,128]{2,1,0:T(4,128)(2,1)S(1)} %squeeze.32), kind=kOutput, calls=%fused_computation.9.clone.1 | convolution fusion | flops 340656128 | bytes 3278081 | tf_op jit(solution)/shard_map/while/body/eval_jaxpr/hck,khe->che/dot_general | solution.py:20
  111.1 2.8 %fusion.22 = (f32[512]{0:T(512)S(1)}, f32[512]{0:T(512)S(1)}, f32[512,4,128]{0,2,1:T(8,128)}) fusion(f32[512,4,128]{0,2,1:T(8,128)} %get-tuple-element.99, f32[512,4,128]{0,2,1:T(8,128)} %bitcast.72, f32[512,4]{0,1:T(4,128)S(1)} %divide_multiply_fusion), kind=kLoop, calls=%fused_computation.52 | loop fusion | flops 1571840 | bytes 3158016 | tf_op jit(solution)/shard_map/reduce_sum | solution.py:83
  113.9 1.6 %copy.53 = f32[1,512,512]{2,1,0:T(8,128)S(1)} copy(f32[1,512,512]{1,2,0:T(8,128)} %bitcast.73) | data formatting | bytes 2097152 | tf_op jit(solution)/shard_map/reshape | solution.py:81
  115.4 3.6 %all-reduce = (f32[512]{0:T(512)S(1)}, f32[512]{0:T(512)S(1)}) all-reduce(f32[512]{0:T(512)S(1)} %get-tuple-element.149, f32[512]{0:T(512)S(1)} %get-tuple-element.148), channel_id=1, replica_groups=mesh['groups'=2,'cache'=4,'req'=2,'rep'=2] {'rep'}, use_global_device_ids=true, to_apply=%region_10.11 | all-reduce | flops 1024 | bytes 8192 | tf_op jit(solution)/shard_map/psum | solution.py:82
  119.0 2.1 %fusion.19 = bf16[1,512,512]{2,1,0:T(8,128)(2,1)} fusion(f32[1,512,512]{2,1,0:T(8,128)S(1)} %copy.53, bf16[512,4,512]{2,0,1:T(8,128)(2,1)} %copy-done.1, f32[512]{0:T(512)S(1)} %copy-done.2, f32[512]{0:T(512)S(1)} %get-tuple-element.169, f32[512]{0:T(512)S(1)} %get-tuple-element.168), kind=kLoop, calls=%fused_computation.29 | loop fusion | flops 1572864 | bytes 2103296 | tf_op jit(solution)/shard_map/convert_element_type | solution.py:88
  (30 shorter events, 0.6 us)
Async XLA Ops:
  0.0 24.1 %copy-start = (bf16[16,2,64,512]{3,2,1,0:T(8,128)(2,1)S(1)}, bf16[16,2,64,512]{3,2,1,0:T(8,128)(2,1)}, u32[]{:S(2)}) copy-start(bf16[16,2,64,512]{3,2,1,0:T(8,128)(2,1)} %param.9) | copy-start | bytes 6291460
  26.5 4.7 %copy-start.3 = (s32[1,16]{1,0:T(1,128)S(1)}, s32[1,16]{1,0:T(1,128)}, u32[]{:S(2)}) copy-start(s32[1,16]{1,0:T(1,128)} %param.12) | copy-start | bytes 196
  26.5 4.7 %copy-start.4 = (s32[1,16]{1,0:T(1,128)S(1)}, s32[1,16]{1,0:T(1,128)}, u32[]{:S(2)}) copy-start(s32[1,16]{1,0:T(1,128)} %param.10) | copy-start | bytes 196
  26.5 63.7 %all-to-all-start = ((bf16[4,5,2,64,512]{4,3,2,1,0:T(8,128)(2,1)}), bf16[4,5,2,64,512]{4,3,2,1,0:T(8,128)(2,1)}, u32[]{:S(2)}, u32[]{:S(2)}) async-start(bf16[4,5,2,64,512]{4,3,2,1,0:T(8,128)(2,1)} %bitcast.71), calls=%async_computation | async-start | bytes 5242880 | tf_op jit(solution)/shard_map/all_to_all | solution.py:68
  34.7 1.4 %copy-start.1 = (bf16[512,4,512]{2,0,1:T(8,128)(2,1)}, bf16[512,4,512]{2,0,1:T(8,128)(2,1)S(1)}, u32[]{:S(2)}) copy-start(bf16[512,4,512]{2,0,1:T(8,128)(2,1)S(1)} %fusion.18) | copy-start | bytes 6291460
  111.1 8.0 %copy-start.2 = (f32[512]{0:T(512)S(1)}, f32[512]{0:T(512)}, u32[]{:S(2)}) copy-start(f32[512]{0:T(512)} %param.13) | copy-start | bytes 6148
where the time goes:
time: 122 us; the launch traced here: 121 us
  waiting for transfers between devices  44.7 us (37%)
  blocking collectives  27.1 us (22%)
  local copies, waits for them, and re-layouts  17.3 us (14%)
  matrix products  14.8 us (12%)
  other arithmetic  12.3 us (10%)
  starting transfers between devices  4.67 us (4%)
    all_to_all x1, waiting for transfers between devices, local(): lax.all_to_all(outgoing, 'cache', split_axis=0, concat_axis=0, tiled=True)  44.7 us
    dot_general x4, matrix products, attend(): jnp.einsum('hck,khe->che', weights, value_rows, preferred_element_type=jn...  14.8 us
    all_gather x1, blocking collectives, local(): lax.all_gather(tile_slot, 'cache', axis=0, tiled=True)  10.2 us
    all_gather x1, blocking collectives, local(): lax.all_gather(tile_owner, 'cache', axis=0, tiled=True)  7.3 us
    all_gather x1, blocking collectives, local(): lax.all_gather(tile_length, 'cache', axis=0, tiled=True)  6 us
    all_to_all x1, starting transfers between devices, local(): lax.all_to_all(outgoing, 'cache', split_axis=0, concat_axis=0, tiled=True)  4.67 us
    squeeze x4, local copies, waits for them, and re-layouts, add_owner(): arrived[owner_index]  4.52 us
    psum x1, blocking collectives, local(): lax.psum((jnp.sum(attended, axis=-1), jnp.sum(attended * attended, axis=-...  3.59 us
  transfers between devices with their start and end apart: 1, of which 1 were waited for; matrix products, arithmetic and copies ran while one was open for 11% of the time, Pallas kernels for 0%

commit v1 on v0

v1 whole, which is shorter than its diff:
```python
import functools
import math

import jax
import jax.numpy as jnp
from jax import lax
from jax.experimental import pallas as pl
from jax.experimental.pallas import tpu as pltpu
from jax.sharding import PartitionSpec as P

D = 1024
HEADS = 8
HEAD = D // HEADS
TILE = 64
HT = 16
HALF_SCALE = 0.5 / math.sqrt(HEAD)
ROWS = 128


def silu_half(half):
    return half + half * jnp.tanh(half)


def kernel(
    n, depth, cand_ref, kv_ref, owner_ref, slot_ref, length_ref, gain_ref, out_ref,
    act, total, stats, peer_stats, table, wanted, wanted_s, own_tiles, outgoing, arrived,
    lens, list_send, list_recv, table_sem, tile_send, tile_recv, stat_send, stat_recv,
):
    me = lax.axis_index("cache")
    core = lax.axis_index("rep")
    cands, width = total.shape
    peers = [lax.rem(me + d, n) for d in range(1, n)]

    barrier = pltpu.get_barrier_semaphore()
    for peer in peers:
        pl.semaphore_signal(
            barrier, inc=1, device_id={"cache": peer}, device_id_type=pl.DeviceIdType.MESH
        )
    pl.semaphore_signal(
        barrier, inc=1, device_id={"rep": 1 - core}, device_id_type=pl.DeviceIdType.MESH
    )

    lane = lax.broadcasted_iota(jnp.int32, (n, 128), 1)
    row = lax.broadcasted_iota(jnp.int32, (n, 128), 0)

    def spread(ref):
        padded = jnp.concatenate([ref[...], jnp.zeros((1, 128 - HT), jnp.int32)], axis=1)
        return jnp.broadcast_to(padded, (n, 128))

    owners, slots, lengths = spread(owner_ref), spread(slot_ref), spread(length_ref)
    owned = ((owners == row) & (lengths > 0)).astype(jnp.int32)
    rank = owned
    for step in (1, 2, 4, 8):
        rank = rank + jnp.where(lane >= step, pltpu.roll(rank, step, 1), 0)
    slot_table = jnp.zeros((n, 128), jnp.int32)
    length_table = jnp.zeros((n, 128), jnp.int32)
    for k in range(depth):
        chosen = (owned > 0) & (rank == k + 1)
        slot_k = jnp.sum(jnp.where(chosen, slots, 0), axis=1, keepdims=True)
        length_k = jnp.sum(jnp.where(chosen, lengths, 0), axis=1, keepdims=True)
        slot_table = jnp.where(lane == k, slot_k, slot_table)
        length_table = jnp.where(lane == k, length_k, length_table)
    for o in range(n):
        table[o] = jnp.broadcast_to(slot_table[o : o + 1], (8, 128))
        lens[o] = jnp.broadcast_to(length_table[o : o + 1], (8, 128))

    pl.semaphore_wait(barrier, n)
    list_copies = []
    for d, peer in enumerate(peers):
        copy = pltpu.make_async_remote_copy(
            src_ref=table.at[peer],
            dst_ref=wanted.at[d],
            send_sem=list_send.at[d],
            recv_sem=list_recv.at[d],
            device_id={"cache": peer},
            device_id_type=pl.DeviceIdType.MESH,
        )
        copy.start()
        list_copies.append(copy)

    tile_copies = {}
    for d, copy in enumerate(list_copies):
        copy.wait_recv()
        to_scalar = pltpu.make_async_copy(wanted.at[d], wanted_s.at[d], table_sem.at[d])
        to_scalar.start()
    own_scalar = pltpu.make_async_copy(table.at[me], wanted_s.at[n - 1], table_sem.at[n - 1])
    own_scalar.start()
    for d in range(n - 1):
        pltpu.make_async_copy(wanted.at[d], wanted_s.at[d], table_sem.at[d]).wait()
    own_scalar.wait()
    for k in range(depth):
        for d in range(n - 1):
            home = lax.rem(me + n - d - 1, n)
            outgoing[k, d] = kv_ref[wanted_s[d, 0, k]]
            copy = pltpu.make_async_remote_copy(
                src_ref=outgoing.at[k, d],
                dst_ref=arrived.at[k, d],
                send_sem=tile_send.at[k, d],
                recv_sem=tile_recv.at[k, d],
                device_id={"cache": home},
                device_id_type=pl.DeviceIdType.MESH,
            )
            copy.start()
            tile_copies[k, d] = copy

    def activate(block, carry):
        rows = pl.ds(pl.multiple_of(block * ROWS, ROWS), ROWS)
        for i in range(4):
            half = cand_ref[0, rows, i, :].astype(jnp.float32) * 0.5
            act[i, rows, :] = silu_half(half).astype(jnp.bfloat16)
        for h in range(width // HEAD):
            cols = slice(h * HEAD, (h + 1) * HEAD)
            query = act[0, rows, cols].astype(jnp.float32)
            key = act[1, rows, cols].astype(jnp.float32)
            value = act[2, rows, cols].astype(jnp.float32)
            score = jnp.sum(query * key, axis=1, keepdims=True)
            total[rows, cols] = silu_half(score * HALF_SCALE) * value
        return carry

    lax.fori_loop(0, cands // ROWS, activate, 0)

    for k in range(depth):
        own_tiles[k] = kv_ref[wanted_s[n - 1, 0, k]]

    position = lax.broadcasted_iota(jnp.int32, (TILE, width), 0)

    def attend(tiles, counts, tile_count):
        for t in range(tile_count):
            live = (position < counts[t]).astype(jnp.float32)
            tiles[t, 0] = (tiles[t, 0].astype(jnp.float32) * live).astype(jnp.bfloat16)

        def one(block, carry):
            rows = pl.ds(pl.multiple_of(block * ROWS, ROWS), ROWS)
            for h in range(width // HEAD):
                cols = slice(h * HEAD, (h + 1) * HEAD)
                keys = tiles[:, 0, :, cols].reshape(tile_count * TILE, HEAD)
                values = tiles[:, 1, :, cols].reshape(tile_count * TILE, HEAD)
                scores = lax.dot_general(
                    act[0, rows, cols], keys, (((1,), (1,)), ((), ())),
                    preferred_element_type=jnp.float32,
                )
                weights = silu_half(scores * HALF_SCALE).astype(jnp.bfloat16)
                total[rows, cols] += jnp.dot(
                    weights, values, preferred_element_type=jnp.float32
                )
            return carry

        lax.fori_loop(0, cands // ROWS, one, 0)

    own_counts = lens[me]
    attend(own_tiles, [own_counts[0:1, k : k + 1] for k in range(depth)], depth)
    for k in range(depth):
        counts = []
        for d in range(n - 1):
            tile_copies[k, d].wait_recv()
            counts.append(lens[lax.rem(me + d + 1, n)][0:1, k : k + 1])
        attend(arrived.at[k], counts, n - 1)

    def moments(block, carry):
        rows = pl.ds(pl.multiple_of(block * ROWS, ROWS), ROWS)
        attended = total[rows, :] * (1.0 / (HT * TILE + 1))
        sums = jnp.sum(attended, axis=1, keepdims=True)
        squares = jnp.sum(attended * attended, axis=1, keepdims=True)
        at = lax.broadcasted_iota(jnp.int32, (ROWS, 128), 1)
        stats[rows, :] = jnp.where(at < 64, sums, squares)
        return carry

    lax.fori_loop(0, cands // ROWS, moments, 0)
    stat_copy = pltpu.make_async_remote_copy(
        src_ref=stats,
        dst_ref=peer_stats,
        send_sem=stat_send,
        recv_sem=stat_recv,
        device_id={"rep": 1 - core},
        device_id_type=pl.DeviceIdType.MESH,
    )
    stat_copy.start()
    stat_copy.wait_recv()

    def finish(block, carry):
        rows = pl.ds(pl.multiple_of(block * ROWS, ROWS), ROWS)
        both = stats[rows, :] + peer_stats[rows, :]
        average = both[:, 0:1] * (1.0 / D)
        spread_ = both[:, 64:65] * (1.0 / D) - average * average
        attended = total[rows, :] * (1.0 / (HT * TILE + 1))
        normed = (attended - average) * lax.rsqrt(spread_ + 1e-05) * gain_ref[...]
        out_ref[0, rows, :] = (normed * act[3, rows, :].astype(jnp.float32)).astype(jnp.bfloat16)
        return carry

    lax.fori_loop(0, cands // ROWS, finish, 0)
    stat_copy.wait_send()
    for copy in list_copies:
        copy.wait_send()
    for copy in tile_copies.values():
        copy.wait_send()


def local(candidates, kv_cache, tile_owner, tile_slot, tile_length, norm_gain):
    n = lax.axis_size("cache")
    depth = (HT - 2) // n + 2
    cands, width = candidates.shape[1], candidates.shape[3]
    vmem = pl.BlockSpec(memory_space=pltpu.VMEM)
    tile = (2, TILE, width)
    dma = pltpu.SemaphoreType.DMA
    return pl.pallas_call(
        functools.partial(kernel, n, depth),
        out_shape=jax.ShapeDtypeStruct((1, cands, width), jnp.bfloat16),
        in_specs=[vmem] * 6,
        out_specs=vmem,
        scratch_shapes=[
            pltpu.VMEM((4, cands, width), jnp.bfloat16),
            pltpu.VMEM((cands, width), jnp.float32),
            pltpu.VMEM((cands, 128), jnp.float32),
            pltpu.VMEM((cands, 128), jnp.float32),
            pltpu.VMEM((n, 8, 128), jnp.int32),
            pltpu.VMEM((n - 1, 8, 128), jnp.int32),
            pltpu.SMEM((n, 8, 128), jnp.int32),
            pltpu.VMEM((depth,) + tile, jnp.bfloat16),
            pltpu.VMEM((depth, n - 1) + tile, jnp.bfloat16),
            pltpu.VMEM((depth, n - 1) + tile, jnp.bfloat16),
            pltpu.VMEM((n, 8, 128), jnp.int32),
            dma((n - 1,)),
            dma((n - 1,)),
            dma((n,)),
            dma((depth, n - 1)),
            dma((depth, n - 1)),
            dma,
            dma,
        ],
        compiler_params=pltpu.CompilerParams(
            collective_id=0, has_side_effects=True, vmem_limit_bytes=48 * 1024 * 1024
        ),
        cost_estimate=pl.CostEstimate(
            flops=4 * cands * width * HT * TILE, bytes_accessed=5 * 2**20, transcendentals=0
        ),
    )(candidates, kv_cache, tile_owner, tile_slot, tile_length, norm_gain[None])


def solution(mesh):
    placed = (
        P(("groups", "cache", "req"), None, None, "rep"),
        P(("groups", "cache", "req"), None, None, "rep"),
        P(("groups", "cache", "req"), None),
        P(("groups", "cache", "req"), None),
        P(("groups", "cache", "req"), None),
        P("rep"),
    )
    return jax.shard_map(
        local,
        mesh=mesh,
        in_specs=placed,
        out_specs=P(("groups", "cache", "req"), None, "rep"),
        check_vma=False,
    )
```

time: 122 us -> 78.7 us (0.65)
  Pallas kernels: 0 us -> 71.8 us
  waiting for transfers between devices: 44.7 us -> 0 us
  blocking collectives: 27.1 us -> 0 us
  matrix products: 14.8 us -> 0 us
  other arithmetic: 12.3 us -> 0 us
  local copies, waits for them, and re-layouts: 17.3 us -> 6.62 us
  starting transfers between devices: 4.67 us -> 0 us
    pallas_call x0 -> x1, Pallas kernels: none -> 71.8 us  [local(): pl.pallas_call(functools.partial(kernel, n, depth), out_shape=jax.ShapeDt...]
    all_to_all x1 -> x0, waiting for transfers between devices: 44.7 us -> none  [local(): lax.all_to_all(outgoing, 'cache', split_axis=0, concat_axis=0, tiled=True)]
    all_gather x3 -> x0, blocking collectives: 23.5 us -> none  [the longest x1 10.2 us: local(): lax.all_gather(tile_slot, 'cache', axis=0, tiled=True)]
    dot_general x4 -> x0, matrix products: 14.8 us -> none  [attend(): jnp.einsum('hck,khe->che', weights, value_rows, preferred_element_type=jn...]
    convert_element_type x9 -> x0, other arithmetic: 6.88 us -> none  [the longest x1 3 us: local(): jax.nn.silu(candidates[0].astype(jnp.float32)).astype(jnp.bfloat16)]
    squeeze x12 -> x0, local copies, waits for them, and re-layouts: 5.19 us -> none  [the longest x4 4.52 us: add_owner(): arrived[owner_index]]
    reduce_sum x4 -> x0, other arithmetic: 5.01 us -> none  [the longest x1 2.8 us: local(): jnp.sum(attended, axis=-1)]
    all_to_all x1 -> x0, starting transfers between devices: 4.67 us -> none  [local(): lax.all_to_all(outgoing, 'cache', split_axis=0, concat_axis=0, tiled=True)]
  transfers between devices with their start and end apart: 1 -> 0, of which waited for: 1 -> 0; matrix products, arithmetic and copies ran while one was open for 11% -> 0% of each run, Pallas kernels for 0% -> 0%
where the time goes in v1:
time: 78.7 us; the launch traced here: 78.5 us
  Pallas kernels  71.8 us (91%)
  local copies, waits for them, and re-layouts  6.62 us (8%)
    pallas_call x1, Pallas kernels, local(): pl.pallas_call(functools.partial(kernel, n, depth), out_shape=jax.ShapeDt...  71.8 us
    unnamed x13, local copies, waits for them, and re-layouts  6.62 us

profile of v1, /device:TPU:1, one launch (start us, length us, event | category | flops | bytes accessed | tf_op | source)
XLA Modules:
  0.0 78.5 jit_solution(14255001479692055766)
XLA Ops:
  0.0 0.0 copy-start
  0.0 1.6 %copy-done = bf16[1,512,4,512]{3,2,1,0:T(4,128)(2,1)S(1)} copy-done((bf16[1,512,4,512]{3,2,1,0:T(4,128)(2,1)S(1)}, bf16[1,512,4,512]{3,2,1,0:T(4,128)(2,1)}, u32[]{:S(2)}) %copy-start) | copy-done | bytes 2097176
  1.6 0.0 copy-start.1
  1.6 1.6 %copy-done.1 = bf16[16,2,64,512]{3,2,1,0:T(8,128)(2,1)S(1)} copy-done((bf16[16,2,64,512]{3,2,1,0:T(8,128)(2,1)S(1)}, bf16[16,2,64,512]{3,2,1,0:T(8,128)(2,1)}, u32[]{:S(2)}) %copy-start.1) | copy-done | bytes 2097176
  3.2 0.0 copy-start.2
  3.2 0.7 copy-done.2
  3.9 0.0 copy-start.3
  3.9 0.7 copy-done.3
  4.5 0.0 copy-start.4
  4.5 0.7 copy-done.4
  5.2 0.0 copy-start.5
  5.2 0.7 copy-done.5
  5.8 71.8 %shard_map.64 = bf16[1,512,512]{2,1,0:T(8,128)(2,1)S(1)} custom-call(bf16[1,512,4,512]{3,2,1,0:T(4,128)(2,1)S(1)} %copy-done, bf16[16,2,64,512]{3,2,1,0:T(8,128)(2,1)S(1)} %copy-done.1, s32[1,16]{1,0:T(1,128)S(1)} %copy-done.3, s32[1,16]{1,0:T(1,128)S(1)} %copy-done.4, s32[1,16]{1,0:T(1,128)S(1)} %copy-done.5, f32[1,512]{1,0:T(1,128)S(1)} %bitcast.1), custom_call_target="tpu_custom_call" | custom-call | flops 1073741824 | bytes 5242880 | tf_op jit(solution)/shard_map/pallas_call | solution.py:205
  77.7 0.8 %copy.8 = bf16[1,512,512]{2,1,0:T(8,128)(2,1)} copy(bf16[1,512,512]{2,1,0:T(8,128)(2,1)S(1)} %shard_map.64) | data formatting | bytes 1048576
Async XLA Ops:
  0.0 1.6 %copy-start = (bf16[1,512,4,512]{3,2,1,0:T(4,128)(2,1)S(1)}, bf16[1,512,4,512]{3,2,1,0:T(4,128)(2,1)}, u32[]{:S(2)}) copy-start(bf16[1,512,4,512]{3,2,1,0:T(4,128)(2,1)} %cand_ref.1) | copy-start | bytes 6291460
  1.6 1.6 %copy-start.1 = (bf16[16,2,64,512]{3,2,1,0:T(8,128)(2,1)S(1)}, bf16[16,2,64,512]{3,2,1,0:T(8,128)(2,1)}, u32[]{:S(2)}) copy-start(bf16[16,2,64,512]{3,2,1,0:T(8,128)(2,1)} %kv_ref.1) | copy-start | bytes 6291460
  3.2 0.7 copy-start.2
  3.9 0.7 copy-start.3
  4.5 0.7 copy-start.4
  5.2 0.7 copy-start.5

commit v2 on v1

v2 whole, which is shorter than its diff:
```python
import functools
import math

import jax
import jax.numpy as jnp
from jax import lax
from jax.experimental import pallas as pl
from jax.experimental.pallas import tpu as pltpu
from jax.sharding import PartitionSpec as P

D = 1024
HEADS = 8
HEAD = D // HEADS
TILE = 64
HT = 16
HALF_SCALE = 0.5 / math.sqrt(HEAD)
ROWS = 128


def silu_half(half):
    return half + half * jnp.tanh(half)


def kernel(
    n, depth, split, cand_hbm, kv_hbm, owner_hbm, slot_hbm, length_hbm, gain_hbm, out_ref,
    cand_ref, kv_ref, lists, gain_ref,
    act, total, stats, peer_stats, table, wanted, wanted_s, own_tiles, outgoing, arrived,
    peer_query, peer_total, partial_out, partial_in,
    load_sem, list_send, list_recv, table_sem, tile_send, tile_recv, stat_send, stat_recv,
    query_send, query_recv, partial_send, partial_recv,
):
    me = lax.axis_index("cache")
    core = lax.axis_index("rep")
    cands, width = total.shape
    peers = [lax.rem(me + d, n) for d in range(1, n)]
    middle = (me + 1) // 2 == 1
    edge = (me + 1) // 2 != 1
    near = 4 - 2 * me

    list_loads = [
        pltpu.make_async_copy(src, lists.at[i], load_sem.at[i])
        for i, src in enumerate((owner_hbm, slot_hbm, length_hbm))
    ]
    cand_load = pltpu.make_async_copy(cand_hbm.at[0], cand_ref, load_sem.at[3])
    kv_load = pltpu.make_async_copy(kv_hbm, kv_ref, load_sem.at[4])
    gain_load = pltpu.make_async_copy(gain_hbm, gain_ref, load_sem.at[5])
    for load in list_loads + [cand_load, kv_load, gain_load]:
        load.start()

    barrier = pltpu.get_barrier_semaphore()
    for peer in peers:
        pl.semaphore_signal(
            barrier, inc=1, device_id={"cache": peer}, device_id_type=pl.DeviceIdType.MESH
        )
    pl.semaphore_signal(
        barrier, inc=1, device_id={"rep": 1 - core}, device_id_type=pl.DeviceIdType.MESH
    )
    for load in list_loads:
        load.wait()

    lane = lax.broadcasted_iota(jnp.int32, (n, 128), 1)
    row = lax.broadcasted_iota(jnp.int32, (n, 128), 0)

    def spread(i):
        padded = jnp.concatenate([lists[i], jnp.zeros((1, 128 - HT), jnp.int32)], axis=1)
        return jnp.broadcast_to(padded, (n, 128))

    owners, slots, lengths = spread(0), spread(1), spread(2)
    owned = ((owners == row) & (lengths > 0) & (lane < HT)).astype(jnp.int32)
    rank = owned
    for step in (1, 2, 4, 8):
        rank = rank + jnp.where(lane >= step, pltpu.roll(rank, step, 1), 0)
    slot_table = jnp.zeros((n, 128), jnp.int32)
    length_table = jnp.zeros((n, 128), jnp.int32)
    for k in range(depth):
        chosen = (owned > 0) & (rank == k + 1)
        slot_k = jnp.sum(jnp.where(chosen, slots, 0), axis=1, keepdims=True)
        length_k = jnp.sum(jnp.where(chosen, lengths, 0), axis=1, keepdims=True)
        slot_table = jnp.where(lane == k, slot_k, slot_table)
        length_table = jnp.where(lane == k, length_k, length_table)
    line = lax.broadcasted_iota(jnp.int32, (8, 128), 0)
    for o in range(n):
        table[o] = jnp.where(line == 0, slot_table[o : o + 1], length_table[o : o + 1])

    pl.semaphore_wait(barrier, n)
    list_copies = []
    for d, peer in enumerate(peers):
        copy = pltpu.make_async_remote_copy(
            src_ref=table,
            dst_ref=wanted.at[d],
            send_sem=list_send.at[d],
            recv_sem=list_recv.at[d],
            device_id={"cache": peer},
            device_id_type=pl.DeviceIdType.MESH,
        )
        copy.start()
        list_copies.append(copy)
    own_scalar = pltpu.make_async_copy(table.at[me], wanted_s.at[n - 1], table_sem.at[n - 1])
    own_scalar.start()

    def activate(parts):
        def one(block, carry):
            rows = pl.ds(pl.multiple_of(block * ROWS, ROWS), ROWS)
            for i in parts:
                half = cand_ref[rows, i, :].astype(jnp.float32) * 0.5
                act[i, rows, :] = silu_half(half).astype(jnp.bfloat16)
            return carry

        lax.fori_loop(0, cands // ROWS, one, 0)

    cand_load.wait()
    query_copy = pltpu.make_async_remote_copy(
        src_ref=act.at[0],
        dst_ref=peer_query,
        send_sem=query_send,
        recv_sem=query_recv,
        device_id={"cache": lax.rem(n + 3 - me, n)},
        device_id_type=pl.DeviceIdType.MESH,
    )
    partial_copy = pltpu.make_async_remote_copy(
        src_ref=partial_out,
        dst_ref=partial_in,
        send_sem=partial_send,
        recv_sem=partial_recv,
        device_id={"cache": lax.rem(n + 3 - me, n)},
        device_id_type=pl.DeviceIdType.MESH,
    )
    if split:
        activate((0,))
        pl.when(middle)(query_copy.start)

    to_scalar = []
    for d, copy in enumerate(list_copies):
        copy.wait_recv()
        move = pltpu.make_async_copy(wanted.at[d, me], wanted_s.at[d], table_sem.at[d])
        move.start()
        to_scalar.append(move)
    kv_load.wait()
    for move in to_scalar:
        move.wait()
    own_scalar.wait()

    def tile_copy(k, d):
        to = lax.rem(me + n - d - 1, n)
        if split and d == 1:
            to = jnp.where(edge, 1 + me // 2, to)
        return pltpu.make_async_remote_copy(
            src_ref=outgoing.at[k, d],
            dst_ref=arrived.at[k, d],
            send_sem=tile_send.at[k, d],
            recv_sem=tile_recv.at[k, d],
            device_id={"cache": to},
            device_id_type=pl.DeviceIdType.MESH,
        )

    def push(k, d):
        outgoing[k, d] = kv_ref[wanted_s[d, 0, k]]
        tile_copy(k, d).start()

    def is_sent(d):
        return jnp.logical_or(me != 1 if d == 2 else me != 2, edge)

    if split:
        for k in range(depth):
            push(k, 1)
        for k in range(depth):
            for d in (0, 2):
                pl.when(is_sent(d))(functools.partial(push, k, d))
    else:
        for k in range(depth):
            for d in range(n - 1):
                push(k, d)

    activate((1, 2, 3) if split else (0, 1, 2, 3))

    def own_term(block, carry):
        rows = pl.ds(pl.multiple_of(block * ROWS, ROWS), ROWS)
        for h in range(width // HEAD):
            cols = slice(h * HEAD, (h + 1) * HEAD)
            query = act[0, rows, cols].astype(jnp.float32)
            key = act[1, rows, cols].astype(jnp.float32)
            value = act[2, rows, cols].astype(jnp.float32)
            score = jnp.sum(query * key, axis=1, keepdims=True)
            total[rows, cols] = silu_half(score * HALF_SCALE) * value
        return carry

    lax.fori_loop(0, cands // ROWS, own_term, 0)
    position = lax.broadcasted_iota(jnp.int32, (TILE, width), 0)

    def attend(query, result, tiles, counts, first=False):
        tile_count = len(counts)
        for t in range(tile_count):
            live = (position < counts[t]).astype(jnp.float32)
            tiles[t, 0] = (tiles[t, 0].astype(jnp.float32) * live).astype(jnp.bfloat16)

        def one(block, carry):
            rows = pl.ds(pl.multiple_of(block * ROWS, ROWS), ROWS)
            for h in range(width // HEAD):
                cols = slice(h * HEAD, (h + 1) * HEAD)
                keys = tiles[:, 0, :, cols].reshape(tile_count * TILE, HEAD)
                values = tiles[:, 1, :, cols].reshape(tile_count * TILE, HEAD)
                scores = lax.dot_general(
                    query[rows, cols], keys, (((1,), (1,)), ((), ())),
                    preferred_element_type=jnp.float32,
                )
                weights = silu_half(scores * HALF_SCALE).astype(jnp.bfloat16)
                added = jnp.dot(weights, values, preferred_element_type=jnp.float32)
                result[rows, cols] = added if first else result[rows, cols] + added
            return carry

        lax.fori_loop(0, cands // ROWS, one, 0)

    def counts_of(ref):
        block = ref[...]
        return [block[1:2, k : k + 1] for k in range(depth)]

    for k in range(depth):
        own_tiles[k] = kv_ref[wanted_s[n - 1, 0, k]]
    attend(act.at[0], total, own_tiles, counts_of(table.at[me]))

    def from_all():
        for k in range(depth):
            counts = []
            for d in range(n - 1):
                tile_copy(k, d).wait_recv()
                counts.append(table[lax.rem(me + d + 1, n)][1:2, k : k + 1])
            attend(act.at[0], total, arrived.at[k], counts)

    def for_both():
        side = 3 * (me - 1)
        for k in range(depth):
            own_tiles[k] = kv_ref[wanted_s[near, 0, k]]
        query_copy.wait_recv()
        attend(peer_query, peer_total, own_tiles, counts_of(wanted.at[near, me]), first=True)
        for k in range(depth):
            tile_copy(k, 1).wait_recv()
        attend(peer_query, peer_total, arrived.at[:, 1], counts_of(wanted.at[near, side]))

        def narrow(block, carry):
            rows = pl.ds(pl.multiple_of(block * ROWS, ROWS), ROWS)
            partial_out[rows, :] = peer_total[rows, :].astype(jnp.bfloat16)
            return carry

        lax.fori_loop(0, cands // ROWS, narrow, 0)
        partial_copy.start()
        for d in (0, 2):

            @pl.when(near == d)
            def _():
                for k in range(depth):
                    tile_copy(k, d).wait_recv()
                attend(act.at[0], total, arrived.at[:, d], counts_of(table.at[side]))

        partial_copy.wait_recv()

        def widen(block, carry):
            rows = pl.ds(pl.multiple_of(block * ROWS, ROWS), ROWS)
            total[rows, :] += partial_in[rows, :].astype(jnp.float32)
            return carry

        lax.fori_loop(0, cands // ROWS, widen, 0)

    if split:
        pl.when(edge)(from_all)
        pl.when(middle)(for_both)
    else:
        from_all()

    gain_load.wait()

    def moments(block, carry):
        rows = pl.ds(pl.multiple_of(block * ROWS, ROWS), ROWS)
        attended = total[rows, :] * (1.0 / (HT * TILE + 1))
        sums = jnp.sum(attended, axis=1, keepdims=True)
        squares = jnp.sum(attended * attended, axis=1, keepdims=True)
        at = lax.broadcasted_iota(jnp.int32, (ROWS, 128), 1)
        stats[rows, :] = jnp.where(at < 64, sums, squares)
        return carry

    lax.fori_loop(0, cands // ROWS, moments, 0)
    stat_copy = pltpu.make_async_remote_copy(
        src_ref=stats,
        dst_ref=peer_stats,
        send_sem=stat_send,
        recv_sem=stat_recv,
        device_id={"rep": 1 - core},
        device_id_type=pl.DeviceIdType.MESH,
    )
    stat_copy.start()
    stat_copy.wait_recv()

    def finish(block, carry):
        rows = pl.ds(pl.multiple_of(block * ROWS, ROWS), ROWS)
        both = stats[rows, :] + peer_stats[rows, :]
        average = both[:, 0:1] * (1.0 / D)
        variance = both[:, 64:65] * (1.0 / D) - average * average
        attended = total[rows, :] * (1.0 / (HT * TILE + 1))
        normed = (attended - average) * lax.rsqrt(variance + 1e-05) * gain_ref[...]
        out_ref[0, rows, :] = (normed * act[3, rows, :].astype(jnp.float32)).astype(jnp.bfloat16)
        return carry

    lax.fori_loop(0, cands // ROWS, finish, 0)
    stat_copy.wait_send()
    for copy in list_copies:
        copy.wait_send()
    for k in range(depth):
        for d in range(n - 1):
            wait = tile_copy(k, d).wait_send
            if split and d != 1:
                pl.when(is_sent(d))(wait)
            else:
                wait()
    if split:

        @pl.when(middle)
        def _():
            query_copy.wait_send()
            partial_copy.wait_send()


def local(candidates, kv_cache, tile_owner, tile_slot, tile_length, norm_gain):
    n = lax.axis_size("cache")
    depth = (HT - 2) // n + 2
    cands, width = candidates.shape[1], candidates.shape[3]
    vmem = pl.BlockSpec(memory_space=pltpu.VMEM)
    tile = (2, TILE, width)
    dma = pltpu.SemaphoreType.DMA
    return pl.pallas_call(
        functools.partial(kernel, n, depth, n == 4),
        out_shape=jax.ShapeDtypeStruct((1, cands, width), jnp.bfloat16),
        in_specs=[pl.BlockSpec(memory_space=pltpu.HBM)] * 6,
        out_specs=vmem,
        scratch_shapes=[
            pltpu.VMEM((cands, 4, width), jnp.bfloat16),
            pltpu.VMEM(kv_cache.shape, jnp.bfloat16),
            pltpu.VMEM((3, 1, HT), jnp.int32),
            pltpu.VMEM((1, width), jnp.float32),
            pltpu.VMEM((4, cands, width), jnp.bfloat16),
            pltpu.VMEM((cands, width), jnp.float32),
            pltpu.VMEM((cands, 128), jnp.float32),
            pltpu.VMEM((cands, 128), jnp.float32),
            pltpu.VMEM((n, 8, 128), jnp.int32),
            pltpu.VMEM((n - 1, n, 8, 128), jnp.int32),
            pltpu.SMEM((n, 8, 128), jnp.int32),
            pltpu.VMEM((depth,) + tile, jnp.bfloat16),
            pltpu.VMEM((depth, n - 1) + tile, jnp.bfloat16),
            pltpu.VMEM((depth, n - 1) + tile, jnp.bfloat16),
            pltpu.VMEM((cands, width), jnp.bfloat16),
            pltpu.VMEM((cands, width), jnp.float32),
            pltpu.VMEM((cands, width), jnp.bfloat16),
            pltpu.VMEM((cands, width), jnp.bfloat16),
            dma((6,)),
            dma((n - 1,)),
            dma((n - 1,)),
            dma((n,)),
            dma((depth, n - 1)),
            dma((depth, n - 1)),
            dma,
            dma,
            dma,
            dma,
            dma,
            dma,
        ],
        compiler_params=pltpu.CompilerParams(
            collective_id=0, has_side_effects=True, vmem_limit_bytes=48 * 1024 * 1024
        ),
        cost_estimate=pl.CostEstimate(
            flops=4 * cands * width * HT * TILE, bytes_accessed=5 * 2**20, transcendentals=0
        ),
    )(candidates, kv_cache, tile_owner, tile_slot, tile_length, norm_gain[None])


def solution(mesh):
    placed = (
        P(("groups", "cache", "req"), None, None, "rep"),
        P(("groups", "cache", "req"), None, None, "rep"),
        P(("groups", "cache", "req"), None),
        P(("groups", "cache", "req"), None),
        P(("groups", "cache", "req"), None),
        P("rep"),
    )
    return jax.shard_map(
        local,
        mesh=mesh,
        in_specs=placed,
        out_specs=P(("groups", "cache", "req"), None, "rep"),
        check_vma=False,
    )
```

time: 78.7 us -> 67.2 us (0.85)
  Pallas kernels: 71.8 us -> 59.7 us
    pallas_call x1, Pallas kernels: 71.8 us -> 59.7 us  [local(): pl.pallas_call(functools.partial(kernel, n, depth, n == 4), out_shape=jax...]
where the time goes in v2:
time: 67.2 us; the launch traced here: 66.4 us
  Pallas kernels  59.7 us (89%)
  local copies, waits for them, and re-layouts  6.62 us (10%)
    pallas_call x1, Pallas kernels, local(): pl.pallas_call(functools.partial(kernel, n, depth, n == 4), out_shape=jax...  59.7 us
    unnamed x13, local copies, waits for them, and re-layouts  6.62 us

profile of v2, /device:TPU:1, one launch (start us, length us, event | category | flops | bytes accessed | tf_op | source)
XLA Modules:
  0.0 66.4 jit_solution(3156611769067393780)
XLA Ops:
  0.0 0.0 copy-start
  0.0 1.6 %copy-done = bf16[1,512,4,512]{3,2,1,0:T(4,128)(2,1)S(1)} copy-done((bf16[1,512,4,512]{3,2,1,0:T(4,128)(2,1)S(1)}, bf16[1,512,4,512]{3,2,1,0:T(4,128)(2,1)}, u32[]{:S(2)}) %copy-start) | copy-done | bytes 2097176
  1.6 0.0 copy-start.1
  1.6 1.6 %copy-done.1 = bf16[16,2,64,512]{3,2,1,0:T(8,128)(2,1)S(1)} copy-done((bf16[16,2,64,512]{3,2,1,0:T(8,128)(2,1)S(1)}, bf16[16,2,64,512]{3,2,1,0:T(8,128)(2,1)}, u32[]{:S(2)}) %copy-start.1) | copy-done | bytes 2097176
  3.2 0.0 copy-start.2
  3.2 0.7 %copy-done.2 = f32[512]{0:T(512)S(1)} copy-done((f32[512]{0:T(512)S(1)}, f32[512]{0:T(512)}, u32[]{:S(2)}) %copy-start.2) | copy-done | bytes 2072
  3.9 0.0 copy-start.3
  3.9 0.7 copy-done.3
  4.5 0.0 copy-start.4
  4.5 0.7 copy-done.4
  5.2 0.0 copy-start.5
  5.2 0.7 copy-done.5
  5.8 59.7 %shard_map.64 = bf16[1,512,512]{2,1,0:T(8,128)(2,1)S(1)} custom-call(bf16[1,512,4,512]{3,2,1,0:T(4,128)(2,1)S(1)} %copy-done, bf16[16,2,64,512]{3,2,1,0:T(8,128)(2,1)S(1)} %copy-done.1, s32[1,16]{1,0:T(1,128)S(1)} %copy-done.3, s32[1,16]{1,0:T(1,128)S(1)} %copy-done.4, s32[1,16]{1,0:T(1,128)S(1)} %copy-done.5, f32[1,512]{1,0:T(1,128)S(1)} %bitcast.1), custom_call_target="tpu_custom_call" | custom-call | flops 1073741824 | bytes 5242880 | tf_op jit(solution)/shard_map/pallas_call | solution.py:328
  65.6 0.8 %copy.8 = bf16[1,512,512]{2,1,0:T(8,128)(2,1)} copy(bf16[1,512,512]{2,1,0:T(8,128)(2,1)S(1)} %shard_map.64) | data formatting | bytes 1048576
Async XLA Ops:
  0.0 1.6 %copy-start = (bf16[1,512,4,512]{3,2,1,0:T(4,128)(2,1)S(1)}, bf16[1,512,4,512]{3,2,1,0:T(4,128)(2,1)}, u32[]{:S(2)}) copy-start(bf16[1,512,4,512]{3,2,1,0:T(4,128)(2,1)} %cand_hbm.1) | copy-start | bytes 6291460
  1.6 1.6 %copy-start.1 = (bf16[16,2,64,512]{3,2,1,0:T(8,128)(2,1)S(1)}, bf16[16,2,64,512]{3,2,1,0:T(8,128)(2,1)}, u32[]{:S(2)}) copy-start(bf16[16,2,64,512]{3,2,1,0:T(8,128)(2,1)} %kv_hbm.1) | copy-start | bytes 6291460
  3.2 0.7 %copy-start.2 = (f32[512]{0:T(512)S(1)}, f32[512]{0:T(512)}, u32[]{:S(2)}) copy-start(f32[512]{0:T(512)} %param.11) | copy-start | bytes 6148
  3.9 0.7 copy-start.3
  4.5 0.7 copy-start.4
  5.2 0.7 copy-start.5

commit v3 on v2

--- a/solution.py
+++ b/solution.py
@@ -363,7 +363,7 @@
             dma,
         ],
         compiler_params=pltpu.CompilerParams(
-            collective_id=0, has_side_effects=True, vmem_limit_bytes=48 * 1024 * 1024
+            collective_id=0, has_side_effects=True, vmem_limit_bytes=60 * 1024 * 1024
         ),
         cost_estimate=pl.CostEstimate(
             flops=4 * cands * width * HT * TILE, bytes_accessed=5 * 2**20, transcendentals=0

time: 67.2 us -> 63 us (0.938)
  local copies, waits for them, and re-layouts: 6.62 us -> 1.87 us
    unnamed x13 -> x1, local copies, waits for them, and re-layouts: 6.62 us -> 1.87 us
where the time goes in v3:
time: 63 us; the launch traced here: 62.1 us
  Pallas kernels  60.3 us (96%)
  local copies, waits for them, and re-layouts  1.87 us (3%)
    pallas_call x1, Pallas kernels, local(): pl.pallas_call(functools.partial(kernel, n, depth, n == 4), out_shape=jax...  60.3 us
    unnamed x1, local copies, waits for them, and re-layouts  1.87 us

profile of v3, /device:TPU:1, one launch (start us, length us, event | category | flops | bytes accessed | tf_op | source)
XLA Modules:
  0.0 62.1 jit_solution(16396209861264620503)
XLA Ops:
  0.0 60.3 %shard_map.64 = bf16[1,512,512]{2,1,0:T(8,128)(2,1)} custom-call(bf16[1,512,4,512]{3,2,1,0:T(4,128)(2,1)} %cand_hbm.1, bf16[16,2,64,512]{3,2,1,0:T(8,128)(2,1)} %kv_hbm.1, s32[1,16]{1,0:T(1,128)} %owner_hbm.1, s32[1,16]{1,0:T(1,128)} %slot_hbm.1, s32[1,16]{1,0:T(1,128)} %length_hbm.1, f32[1,512]{1,0:T(1,128)} %bitcast.1), custom_call_target="tpu_custom_call" | custom-call | flops 1073741824 | bytes 5242880 | tf_op jit(solution)/shard_map/pallas_call | solution.py:328
  60.3 1.9 %copy.8 = bf16[1,512,512]{2,1,0:T(8,128)(2,1)} copy(bf16[1,512,512]{2,1,0:T(8,128)(2,1)} %shard_map.64) | data formatting | bytes 1048576

commit v4 on v3

--- a/solution.py
+++ b/solution.py
@@ -25,9 +25,9 @@
     n, depth, split, cand_hbm, kv_hbm, owner_hbm, slot_hbm, length_hbm, gain_hbm, out_ref,
     cand_ref, kv_ref, lists, gain_ref,
     act, total, stats, peer_stats, table, wanted, wanted_s, own_tiles, outgoing, arrived,
-    peer_query, peer_total, partial_out, partial_in,
+    peer_query, peer_total, partial_out, partial_in, low_arrived,
     load_sem, list_send, list_recv, table_sem, tile_send, tile_recv, stat_send, stat_recv,
-    query_send, query_recv, partial_send, partial_recv,
+    query_send, query_recv, partial_send, partial_recv, low_send, low_recv,
 ):
     me = lax.axis_index("cache")
     core = lax.axis_index("rep")
@@ -36,6 +36,8 @@
     middle = (me + 1) // 2 == 1
     edge = (me + 1) // 2 != 1
     near = 4 - 2 * me
+    facing = 2 * (me // 3)
+    half_width = width // 2
 
     list_loads = [
         pltpu.make_async_copy(src, lists.at[i], load_sem.at[i])
@@ -109,25 +111,29 @@
         lax.fori_loop(0, cands // ROWS, one, 0)
 
     cand_load.wait()
-    query_copy = pltpu.make_async_remote_copy(
-        src_ref=act.at[0],
-        dst_ref=peer_query,
-        send_sem=query_send,
-        recv_sem=query_recv,
-        device_id={"cache": lax.rem(n + 3 - me, n)},
-        device_id_type=pl.DeviceIdType.MESH,
-    )
-    partial_copy = pltpu.make_async_remote_copy(
-        src_ref=partial_out,
-        dst_ref=partial_in,
-        send_sem=partial_send,
-        recv_sem=partial_recv,
-        device_id={"cache": lax.rem(n + 3 - me, n)},
-        device_id_type=pl.DeviceIdType.MESH,
-    )
+    def to_partner(src, dst, send_sem, recv_sem):
+        return pltpu.make_async_remote_copy(
+            src_ref=src,
+            dst_ref=dst,
+            send_sem=send_sem,
+            recv_sem=recv_sem,
+            device_id={"cache": lax.rem(n + 3 - me, n)},
+            device_id_type=pl.DeviceIdType.MESH,
+        )
+
+    def query_copy(cols):
+        return to_partner(act.at[0, :, cols], peer_query.at[:, cols], query_send, query_recv)
+
+    def partial_copy(cols):
+        return to_partner(
+            partial_out.at[:, cols], partial_in.at[:, cols], partial_send, partial_recv
+        )
+
+    every, low, high = slice(0, width), slice(0, half_width), slice(half_width, width)
     if split:
         activate((0,))
-        pl.when(middle)(query_copy.start)
+        pl.when(middle)(query_copy(every).start)
+        pl.when(edge)(query_copy(low).start)
 
     to_scalar = []
     for d, copy in enumerate(list_copies):
@@ -140,32 +146,63 @@
         move.wait()
     own_scalar.wait()
 
-    def tile_copy(k, d):
+    def tile_copy(k, d, cols=every):
         to = lax.rem(me + n - d - 1, n)
         if split and d == 1:
             to = jnp.where(edge, 1 + me // 2, to)
         return pltpu.make_async_remote_copy(
-            src_ref=outgoing.at[k, d],
-            dst_ref=arrived.at[k, d],
+            src_ref=outgoing.at[k, d, :, :, cols],
+            dst_ref=arrived.at[k, d, :, :, cols],
             send_sem=tile_send.at[k, d],
             recv_sem=tile_recv.at[k, d],
             device_id={"cache": to},
             device_id_type=pl.DeviceIdType.MESH,
         )
 
-    def push(k, d):
+    def low_copy(k):
+        return pltpu.make_async_remote_copy(
+            src_ref=outgoing.at[k, 1, :, :, low],
+            dst_ref=low_arrived.at[k],
+            send_sem=low_send.at[k],
+            recv_sem=low_recv.at[k],
+            device_id={"cache": jnp.where(me == 1, 0, n - 1)},
+            device_id_type=pl.DeviceIdType.MESH,
+        )
+
+    def push(k, d, cols=every):
         outgoing[k, d] = kv_ref[wanted_s[d, 0, k]]
-        tile_copy(k, d).start()
-
-    def is_sent(d):
-        return jnp.logical_or(me != 1 if d == 2 else me != 2, edge)
+        tile_copy(k, d, cols).start()
+
+    def push_low(k):
+        outgoing[k, 1] = kv_ref[wanted_s[1, 0, k]]
+        low_copy(k).start()
+
+    def sends(d, action):
+        if d == 1:
+            pl.when(edge)(functools.partial(action, 1, every))
+            pl.when(middle)(functools.partial(action, 1, high))
+        else:
+            pl.when(jnp.logical_and(middle, near != d))(functools.partial(action, d, every))
+            pl.when(jnp.logical_and(edge, facing != d))(functools.partial(action, d, every))
+            pl.when(jnp.logical_and(edge, facing == d))(functools.partial(action, d, high))
 
     if split:
-        for k in range(depth):
-            push(k, 1)
+
+        @pl.when(middle)
+        def _():
+            for k in range(depth):
+                push_low(k)
+            for k in range(depth):
+                tile_copy(k, 1, high).start()
+
+        @pl.when(edge)
+        def _():
+            for k in range(depth):
+                push(k, 1)
+
         for k in range(depth):
             for d in (0, 2):
-                pl.when(is_sent(d))(functools.partial(push, k, d))
+                sends(d, lambda d, cols, k=k: push(k, d, cols))
     else:
         for k in range(depth):
             for d in range(n - 1):
@@ -187,15 +224,21 @@
     lax.fori_loop(0, cands // ROWS, own_term, 0)
     position = lax.broadcasted_iota(jnp.int32, (TILE, width), 0)
 
-    def attend(query, result, tiles, counts, first=False):
+    def attend(query, result, tiles, counts, first=False, heads=None, clean=True):
         tile_count = len(counts)
-        for t in range(tile_count):
-            live = (position < counts[t]).astype(jnp.float32)
-            tiles[t, 0] = (tiles[t, 0].astype(jnp.float32) * live).astype(jnp.bfloat16)
+        heads = range(width // HEAD) if heads is None else heads
+        span = slice(0, width if len(heads) * HEAD == width else half_width)
+        if heads[0] > 0:
+            span = high
+        for t in range(tile_count if clean else 0):
+            live = (position[:, span] < counts[t]).astype(jnp.float32)
+            tiles[t, 0, :, span] = (
+                tiles[t, 0, :, span].astype(jnp.float32) * live
+            ).astype(jnp.bfloat16)
 
         def one(block, carry):
             rows = pl.ds(pl.multiple_of(block * ROWS, ROWS), ROWS)
-            for h in range(width // HEAD):
+            for h in heads:
                 cols = slice(h * HEAD, (h + 1) * HEAD)
                 keys = tiles[:, 0, :, cols].reshape(tile_count * TILE, HEAD)
                 values = tiles[:, 1, :, cols].reshape(tile_count * TILE, HEAD)
@@ -226,23 +269,39 @@
                 counts.append(table[lax.rem(me + d + 1, n)][1:2, k : k + 1])
             attend(act.at[0], total, arrived.at[k], counts)
 
-    def for_both():
-        side = 3 * (me - 1)
-        for k in range(depth):
-            own_tiles[k] = kv_ref[wanted_s[near, 0, k]]
-        query_copy.wait_recv()
-        attend(peer_query, peer_total, own_tiles, counts_of(wanted.at[near, me]), first=True)
-        for k in range(depth):
-            tile_copy(k, 1).wait_recv()
-        attend(peer_query, peer_total, arrived.at[:, 1], counts_of(wanted.at[near, side]))
+    def serve(mine, tiles, side, slot, cols, heads):
+        for k in range(depth):
+            own_tiles[k] = kv_ref[wanted_s[slot, 0, k]]
+        query_copy(cols).wait_recv()
+        attend(peer_query, peer_total, own_tiles, counts_of(mine), first=True, heads=heads)
+        for k in range(depth):
+            if cols is every:
+                tile_copy(k, 1).wait_recv()
+            else:
+                low_copy(k).wait_recv()
+        attend(peer_query, peer_total, tiles, counts_of(wanted.at[slot, side]), heads=heads)
 
         def narrow(block, carry):
             rows = pl.ds(pl.multiple_of(block * ROWS, ROWS), ROWS)
-            partial_out[rows, :] = peer_total[rows, :].astype(jnp.bfloat16)
+            partial_out[rows, cols] = peer_total[rows, cols].astype(jnp.bfloat16)
             return carry
 
         lax.fori_loop(0, cands // ROWS, narrow, 0)
-        partial_copy.start()
+        partial_copy(cols).start()
+
+    def collect(cols):
+        partial_copy(cols).wait_recv()
+
+        def widen(block, carry):
+            rows = pl.ds(pl.multiple_of(block * ROWS, ROWS), ROWS)
+            total[rows, cols] += partial_in[rows, cols].astype(jnp.float32)
+            return carry
+
+        lax.fori_loop(0, cands // ROWS, widen, 0)
+
+    def at_middle():
+        side = 3 * (me - 1)
+        serve(wanted.at[near, me], arrived.at[:, 1], side, near, every, None)
         for d in (0, 2):
 
             @pl.when(near == d)
@@ -251,18 +310,35 @@
                     tile_copy(k, d).wait_recv()
                 attend(act.at[0], total, arrived.at[:, d], counts_of(table.at[side]))
 
-        partial_copy.wait_recv()
-
-        def widen(block, carry):
-            rows = pl.ds(pl.multiple_of(block * ROWS, ROWS), ROWS)
-            total[rows, :] += partial_in[rows, :].astype(jnp.float32)
-            return carry
-
-        lax.fori_loop(0, cands // ROWS, widen, 0)
+        collect(every)
+
+    def at_edge():
+        side = 1 + me // 3
+        lows, highs = (0, 1), (2, 3)
+        serve(wanted.at[facing, me], low_arrived, side, facing, low, lows)
+        for k in range(depth):
+            counts = []
+            for d in range(n - 1):
+                if d == 1:
+                    tile_copy(k, d, high).wait_recv()
+                else:
+                    pl.when(facing == d)(tile_copy(k, d).wait_recv)
+                    pl.when(facing != d)(tile_copy(k, d, high).wait_recv)
+                counts.append(table[lax.rem(me + d + 1, n)][1:2, k : k + 1])
+            attend(act.at[0], total, arrived.at[k], counts, heads=highs)
+            for d in (0, 2):
+
+                @pl.when(facing == d)
+                def _():
+                    attend(
+                        act.at[0], total, arrived.at[k, d : d + 1], counts[d : d + 1], heads=lows
+                    )
+
+        collect(low)
 
     if split:
-        pl.when(edge)(from_all)
-        pl.when(middle)(for_both)
+        pl.when(edge)(at_edge)
+        pl.when(middle)(at_middle)
     else:
         from_all()
 
@@ -303,19 +379,26 @@
     stat_copy.wait_send()
     for copy in list_copies:
         copy.wait_send()
-    for k in range(depth):
-        for d in range(n - 1):
-            wait = tile_copy(k, d).wait_send
-            if split and d != 1:
-                pl.when(is_sent(d))(wait)
-            else:
-                wait()
     if split:
+        for k in range(depth):
+            for d in range(n - 1):
+                sends(d, lambda d, cols, k=k: tile_copy(k, d, cols).wait_send())
 
         @pl.when(middle)
         def _():
-            query_copy.wait_send()
-            partial_copy.wait_send()
+            for k in range(depth):
+                low_copy(k).wait_send()
+            query_copy(every).wait_send()
+            partial_copy(every).wait_send()
+
+        @pl.when(edge)
+        def _():
+            query_copy(low).wait_send()
+            partial_copy(low).wait_send()
+    else:
+        for k in range(depth):
+            for d in range(n - 1):
+                tile_copy(k, d).wait_send()
 
 
 def local(candidates, kv_cache, tile_owner, tile_slot, tile_length, norm_gain):
@@ -349,6 +432,7 @@
             pltpu.VMEM((cands, width), jnp.float32),
             pltpu.VMEM((cands, width), jnp.bfloat16),
             pltpu.VMEM((cands, width), jnp.bfloat16),
+            pltpu.VMEM((depth, 2, TILE, width // 2), jnp.bfloat16),
             dma((6,)),
             dma((n - 1,)),
             dma((n - 1,)),
@@ -361,6 +445,8 @@
             dma,
             dma,
             dma,
+            dma((depth,)),
+            dma((depth,)),
         ],
         compiler_params=pltpu.CompilerParams(
             collective_id=0, has_side_effects=True, vmem_limit_bytes=60 * 1024 * 1024

time: 63 us -> 61.8 us (0.981); the launches traced: 62.1 us -> 61.7 us
  no operation moved by 1% of the time
where the time goes in v4:
time: 61.8 us; the launch traced here: 61.7 us
  Pallas kernels  59.8 us (97%)
  local copies, waits for them, and re-layouts  1.87 us (3%)
    pallas_call x1, Pallas kernels, local(): pl.pallas_call(functools.partial(kernel, n, depth, n == 4), out_shape=jax...  59.8 us
    unnamed x1, local copies, waits for them, and re-layouts  1.87 us

profile of v4, /device:TPU:1, one launch (start us, length us, event | category | flops | bytes accessed | tf_op | source)
XLA Modules:
  0.0 61.7 jit_solution(5743545537178885832)
XLA Ops:
  0.0 59.8 %shard_map.64 = bf16[1,512,512]{2,1,0:T(8,128)(2,1)} custom-call(bf16[1,512,4,512]{3,2,1,0:T(4,128)(2,1)} %cand_hbm.1, bf16[16,2,64,512]{3,2,1,0:T(8,128)(2,1)} %kv_hbm.1, s32[1,16]{1,0:T(1,128)} %owner_hbm.1, s32[1,16]{1,0:T(1,128)} %slot_hbm.1, s32[1,16]{1,0:T(1,128)} %length_hbm.1, f32[1,512]{1,0:T(1,128)} %bitcast.1), custom_call_target="tpu_custom_call" | custom-call | flops 1073741824 | bytes 5242880 | tf_op jit(solution)/shard_map/pallas_call | solution.py:411
  59.8 1.9 %copy.8 = bf16[1,512,512]{2,1,0:T(8,128)(2,1)} copy(bf16[1,512,512]{2,1,0:T(8,128)(2,1)} %shard_map.64) | data formatting | bytes 1048576

commit v5 on v4

--- a/solution.py
+++ b/solution.py
@@ -202,7 +202,12 @@
 
         for k in range(depth):
             for d in (0, 2):
-                sends(d, lambda d, cols, k=k: push(k, d, cols))
+                far = jnp.logical_and(edge, facing == d)
+                pl.when(far)(functools.partial(push, k, d, high))
+        for k in range(depth):
+            for d in (0, 2):
+                close = jnp.where(edge, facing != d, near != d)
+                pl.when(close)(functools.partial(push, k, d))
     else:
         for k in range(depth):
             for d in range(n - 1):

time: 61.8 us -> 63.3 us (1.024)
  Pallas kernels: 59.8 us -> 61.3 us
    pallas_call x1, Pallas kernels: 59.8 us -> 61.3 us  [local(): pl.pallas_call(functools.partial(kernel, n, depth, n == 4), out_shape=jax...]
where the time goes in v5:
time: 63.3 us; the launch traced here: 63.2 us
  Pallas kernels  61.3 us (97%)
  local copies, waits for them, and re-layouts  1.87 us (3%)
    pallas_call x1, Pallas kernels, local(): pl.pallas_call(functools.partial(kernel, n, depth, n == 4), out_shape=jax...  61.3 us
    unnamed x1, local copies, waits for them, and re-layouts  1.87 us

profile of v5, /device:TPU:1, one launch (start us, length us, event | category | flops | bytes accessed | tf_op | source)
XLA Modules:
  0.0 63.2 jit_solution(1831719266270083124)
XLA Ops:
  0.0 61.3 %shard_map.64 = bf16[1,512,512]{2,1,0:T(8,128)(2,1)} custom-call(bf16[1,512,4,512]{3,2,1,0:T(4,128)(2,1)} %cand_hbm.1, bf16[16,2,64,512]{3,2,1,0:T(8,128)(2,1)} %kv_hbm.1, s32[1,16]{1,0:T(1,128)} %owner_hbm.1, s32[1,16]{1,0:T(1,128)} %slot_hbm.1, s32[1,16]{1,0:T(1,128)} %length_hbm.1, f32[1,512]{1,0:T(1,128)} %bitcast.1), custom_call_target="tpu_custom_call" | custom-call | flops 1073741824 | bytes 5242880 | tf_op jit(solution)/shard_map/pallas_call | solution.py:416
  61.3 1.9 %copy.8 = bf16[1,512,512]{2,1,0:T(8,128)(2,1)} copy(bf16[1,512,512]{2,1,0:T(8,128)(2,1)} %shard_map.64) | data formatting | bytes 1048576

commit v6 on v4

--- a/solution.py
+++ b/solution.py
@@ -192,8 +192,9 @@
         def _():
             for k in range(depth):
                 push_low(k)
-            for k in range(depth):
                 tile_copy(k, 1, high).start()
+                for d in (0, 2):
+                    pl.when(near != d)(functools.partial(push, k, d))
 
         @pl.when(edge)
         def _():
@@ -202,7 +203,8 @@
 
         for k in range(depth):
             for d in (0, 2):
-                sends(d, lambda d, cols, k=k: push(k, d, cols))
+                pl.when(edge & (facing != d))(functools.partial(push, k, d))
+                pl.when(edge & (facing == d))(functools.partial(push, k, d, high))
     else:
         for k in range(depth):
             for d in range(n - 1):

time: 61.8 us -> 72.9 us (1.18)
  Pallas kernels: 59.8 us -> 70.8 us
    pallas_call x1, Pallas kernels: 59.8 us -> 70.8 us  [local(): pl.pallas_call(functools.partial(kernel, n, depth, n == 4), out_shape=jax...]
where the time goes in v6:
time: 72.9 us; the launch traced here: 72.7 us
  Pallas kernels  70.8 us (97%)
  local copies, waits for them, and re-layouts  1.87 us (3%)
    pallas_call x1, Pallas kernels, local(): pl.pallas_call(functools.partial(kernel, n, depth, n == 4), out_shape=jax...  70.8 us
    unnamed x1, local copies, waits for them, and re-layouts  1.87 us

profile of v6, /device:TPU:1, one launch (start us, length us, event | category | flops | bytes accessed | tf_op | source)
XLA Modules:
  0.0 72.7 jit_solution(2934245227000567773)
XLA Ops:
  0.0 70.8 %shard_map.64 = bf16[1,512,512]{2,1,0:T(8,128)(2,1)} custom-call(bf16[1,512,4,512]{3,2,1,0:T(4,128)(2,1)} %cand_hbm.1, bf16[16,2,64,512]{3,2,1,0:T(8,128)(2,1)} %kv_hbm.1, s32[1,16]{1,0:T(1,128)} %owner_hbm.1, s32[1,16]{1,0:T(1,128)} %slot_hbm.1, s32[1,16]{1,0:T(1,128)} %length_hbm.1, f32[1,512]{1,0:T(1,128)} %bitcast.1), custom_call_target="tpu_custom_call" | custom-call | flops 1073741824 | bytes 5242880 | tf_op jit(solution)/shard_map/pallas_call | solution.py:413
  70.8 1.9 %copy.8 = bf16[1,512,512]{2,1,0:T(8,128)(2,1)} copy(bf16[1,512,512]{2,1,0:T(8,128)(2,1)} %shard_map.64) | data formatting | bytes 1048576
